TPU v7x, 32 devices: a whole 2x2x4 slice. The times are simulated.
32 devices in a mesh: parts: 2 (over x), tensor: 16 (over z, y, core).
Axes of the slice: x: 2, y: 2, z: 4, core: 2. Of those that a mesh axis runs over, the one named last changes fastest.
Arguments:
- layer_input: bfloat16 [2048, 5120], P('parts', 'tensor'), parts along dimension 0, may hold values from -6 to 6
- out_grad: bfloat16 [2048, 5120], P('parts', 'tensor'), parts along dimension 0, may hold values from -6 to 6
- gate_pre: bfloat16 [2048, 27648], P('parts', 'tensor'), parts along dimension 0, may hold values from -6 to 6
- up_pre: bfloat16 [2048, 27648], P('parts', 'tensor'), parts along dimension 0, may hold values from -6 to 6
- down_weight: bfloat16 [27648, 5120], P('tensor'), may hold values from -0.0390625 to 0.0390625
- proj_input: int32 [5120, 64], P('tensor'), may hold values from -1 to 1
- proj_output: int32 [5120, 64], P('tensor'), may hold values from -1 to 1
- proj_hidden: int32 [27648, 64], P('tensor'), may hold values from -1 to 1
- proj_upgrad: int32 [27648, 64], P('tensor'), may hold values from -1 to 1
- queries: bfloat16 [4096, 8192], P('tensor'), may hold values from -0.059814453 to 0.059814453
- example_ids: int32 [2048], P('parts'), parts along dimension 0, may hold values from 0 to 127, never falling along the last dimension, each value on 1 to 16 neighbouring positions
Outputs:
- scores: float32 [256, 4096], P('parts', 'tensor'), parts along dimension 0
There are 2 independent parts, one for each index of `parts`. A program takes and returns all parts, laid end to end along the dimension named above; an argument that names none is the same for every part. Nothing has to cross between parts.
Inputs may be any that keep to these rules, and one draw needn't show every extreme that they name: `proj_input`: values -1, 0 and 1. `proj_output`: values -1, 0 and 1. `proj_hidden`: values -1, 0 and 1. `proj_upgrad`: values -1, 0 and 1. `example_ids`: ids are non-decreasing along the rows; every example 0..127 holds 1 to 16 contiguous rows, and one holds exactly 16.
All inputs are finite; a program needn't handle non-finite values.
Results may differ from a plain program's by a relative error of at most 0.01.
Values may be sent and summed in bfloat16 or wider, within the bound.
A program may use at most 128 MiB of HBM per device.

v0:
```python
import jax
import jax.numpy as jnp
from jax import lax
from jax.sharding import PartitionSpec as P

D = 5120
FF = 27648
RANK = 64
EXAMPLES = 128


def factor_scales(rank):
    return jnp.concatenate(
        [
            jnp.full((rank,), (1.5 / D) ** 0.5, jnp.float32),
            jnp.full((rank,), (1.5 / FF) ** 0.5, jnp.float32),
            jnp.full((rank,), (1.5 / FF) ** 0.5, jnp.float32),
            jnp.full((rank,), (1.5 / D) ** 0.5, jnp.float32),
        ]
    )


def kron_rows(factors):
    rank = factors.shape[1] // 4
    count = factors.shape[0]
    wide = factors.astype(jnp.float32)
    a_input = wide[:, :rank]
    a_hidden = wide[:, rank : 2 * rank]
    b_upgrad = wide[:, 2 * rank : 3 * rank]
    b_output = wide[:, 3 * rank :]
    up_part = (a_input[:, :, None] * b_upgrad[:, None, :]).reshape(count, rank * rank)
    down_part = (a_hidden[:, :, None] * b_output[:, None, :]).reshape(count, rank * rank)
    return jnp.concatenate([up_part, down_part], 1).astype(jnp.bfloat16)


def per_device(
    layer_input,
    out_grad,
    gate_pre,
    up_pre,
    down_weight,
    proj_input,
    proj_output,
    proj_hidden,
    proj_upgrad,
    queries,
    example_ids,
):
    hidden_grad = lax.dot_general(
        lax.all_gather(out_grad, "tensor", axis=1, tiled=True),
        down_weight,
        (((1,), (1,)), ((), ())),
        preferred_element_type=jnp.float32,
    )
    gate_act = jax.nn.silu(gate_pre.astype(jnp.float32))
    hidden = (gate_act * up_pre.astype(jnp.float32)).astype(jnp.bfloat16)
    up_grad = (hidden_grad * gate_act).astype(jnp.bfloat16)
    partial_value = jnp.concatenate(
        [
            jnp.dot(
                layer_input, proj_input.astype(jnp.bfloat16), preferred_element_type=jnp.float32
            ),
            jnp.dot(hidden, proj_hidden.astype(jnp.bfloat16), preferred_element_type=jnp.float32),
            jnp.dot(up_grad, proj_upgrad.astype(jnp.bfloat16), preferred_element_type=jnp.float32),
            jnp.dot(out_grad, proj_output.astype(jnp.bfloat16), preferred_element_type=jnp.float32),
        ],
        1,
    )
    scales = factor_scales(RANK)
    summed = lax.psum(partial_value, "tensor")
    rows_all = kron_rows((summed * scales).astype(jnp.bfloat16))
    row_scores = lax.dot_general(
        rows_all, queries, (((1,), (1,)), ((), ())), preferred_element_type=jnp.float32
    )
    onehot = (example_ids[None, :] == jnp.arange(EXAMPLES, dtype=jnp.int32)[:, None]).astype(
        jnp.float32
    )
    return jnp.dot(onehot, row_scores, precision=lax.Precision.HIGHEST)


def solution(mesh):
    placed = (
        P("parts", "tensor"),
        P("parts", "tensor"),
        P("parts", "tensor"),
        P("parts", "tensor"),
        P("tensor", None),
        P("tensor", None),
        P("tensor", None),
        P("tensor", None),
        P("tensor", None),
        P("tensor", None),
        P("parts"),
    )
    return jax.shard_map(
        per_device, mesh=mesh, in_specs=placed, out_specs=P("parts", "tensor"), check_vma=False
    )
```

profile of v0, /device:TPU:0, one launch (start us, length us, event | category | flops | bytes accessed | tf_op | source)
XLA Modules:
  0.0 253.2 jit_solution(13104318101754957917)
XLA Ops:
  6.5 0.0 copy-start
  6.5 0.0 all-gather.2.cloned.1.call-start
  6.5 0.7 all-gather.2.cloned.1.call-update
  7.3 0.0 all-reduce.2.cloned.1.call-start
  7.3 1.4 fusion.14
  8.7 0.0 copy-done
  8.7 1.1 fusion.16
  9.9 0.0 copy-start.3
  9.9 5.5 %fusion.7 = f32[1024,64]{0,1:T(8,128)S(1)} fusion(bf16[1024,1728]{0,1:T(8,128)(2,1)} %param.14, bf16[1024,1728]{0,1:T(8,128)(2,1)} %param.13, s32[1728,64]{0,1:T(8,128)} %param.18), kind=kOutput, calls=%fused_computation.13 | convolution fusion | flops 240758784 | bytes 7782400 | tf_op jit(solution)/shard_map/dot_general | solution.py:63
  15.4 0.0 copy-start.2
  15.4 84.8 %all-gather.2.cloned.1.call-done = bf16[1024,5120]{0,1:T(8,128)(2,1)} async-done(((bf16[1024,320]{0,1:T(8,128)(2,1)}), bf16[1024,5120]{0,1:T(8,128)(2,1)}) %all-gather.2.cloned.1.call-update) | async-done | bytes 10485776 | tf_op jit(solution)/shard_map/all_gather | solution.py:50
  100.3 0.0 copy-done.3
  100.3 28.8 %fusion.8 = f32[1024,64]{0,1:T(8,128)S(1)} fusion(bf16[1728,5120]{1,0:T(8,128)(2,1)} %param.15, bf16[1024,5120]{0,1:T(8,128)(2,1)} %all-gather.2.cloned.1.call-done, bf16[1024,1728]{0,1:T(8,128)(2,1)} %param.13, s32[1728,64]{0,1:T(8,128)S(1)} %copy-done.3), kind=kOutput, calls=%fused_computation.14 | convolution fusion | flops 18358382592 | bytes 32423936 | tf_op jit(solution)/shard_map/dot_general | solution.py:64
  129.1 1.1 pad_maximum_fusion
  130.2 0.0 all-reduce.2.cloned.1.call-update
  130.2 91.7 %all-reduce.2.cloned.1.call-done = f32[1024,256]{0,1:T(8,128)} async-done(((f32[1024,256]{0,1:T(8,128)}), f32[1024,256]{0,1:T(8,128)}) %all-reduce.2.cloned.1.call-update) | async-done | bytes 1048592 | tf_op jit(solution)/shard_map/psum | solution.py:70
  221.9 0.0 copy-done.2
  221.9 1.4 fusion.9
  223.3 0.1 fusion.21
  223.4 12.2 %multiply_convert_fusion = (bf16[1024,64,64]{0,2,1:T(8,128)(2,1)}, bf16[1024,64,64]{0,2,1:T(8,128)(2,1)}) fusion(f32[1024,64]{0,1:T(8,128)S(1)} %get-tuple-element.6, f32[1024,64]{0,1:T(8,128)S(1)} %get-tuple-element.7, f32[1024,64]{0,1:T(8,128)S(1)} %get-tuple-element.8, f32[1024,64]{0,1:T(8,128)S(1)} %get-tuple-element.5), kind=kLoop, calls=%fused_computation.4 | loop fusion | flops 16777216 | bytes 17825792 | tf_op jit(solution)/shard_map/convert.2
  235.6 0.0 copy-start.1
  235.6 9.5 %fusion = f32[1024,256]{1,0:T(8,128)S(1)} fusion(bf16[256,8192]{1,0:T(8,128)(2,1)} %param.20, bf16[1024,4096]{0,1:T(8,128)(2,1)} %bitcast.8, bf16[1024,4096]{0,1:T(8,128)(2,1)} %bitcast.9), kind=kOutput, calls=%fused_computation | convolution fusion | flops 4328521728 | bytes 22020096 | tf_op jit(solution)/shard_map/dot_general | solution.py:72
  245.1 0.0 copy-done.1
  245.1 1.2 fusion.10
Async XLA Ops:
  6.5 2.2 copy-start
  6.5 93.7 %all-gather.2.cloned.1.call-start = ((), (), s32[]{:S(2)}) async-start(), calls=%async_computation | async-start | bytes 11141120 | tf_op jit(solution)/shard_map/all_gather | solution.py:50
  7.3 214.6 %all-reduce.2.cloned.1.call-start = ((), (), s32[]{:S(2)}) async-start(), calls=%async_computation.1 | async-start | bytes 2097152 | tf_op jit(solution)/shard_map/psum | solution.py:70
  9.9 90.4 %copy-start.3 = (s32[1728,64]{0,1:T(8,128)S(1)}, s32[1728,64]{0,1:T(8,128)}, u32[]{:S(2)}) copy-start(s32[1728,64]{0,1:T(8,128)} %param.19) | copy-start | bytes 1327108
  15.4 206.5 %copy-start.2 = (f32[256]{0:T(256)S(1)}, f32[256]{0:T(256)}, u32[]{:S(2)}) copy-start(f32[256]{0:T(256)} %constant.5.clone.1) | copy-start | bytes 3076
  235.6 9.5 %copy-start.1 = (s32[1024]{0:T(1024)S(1)}, s32[1024]{0:T(1024)}, u32[]{:S(2)}) copy-start(s32[1024]{0:T(1024)} %param.21) | copy-start | bytes 12292
Sparse Core Ops, SparseCore 0:
  9.6 90.5 all-gather.1
  130.3 91.5 all-reduce.1
where the time goes:
time: 253 us
  waiting for transfers between devices  177 us (70%)
  matrix products  47.6 us (19%)
  other arithmetic  14.7 us (6%)
  between operations  13.5 us (5%)
    psum x1, waiting for transfers between devices, per_device(): summed = lax.psum(partial_value, 'tensor')  91.7 us
    all_gather x1, waiting for transfers between devices, per_device(): lax.all_gather(out_grad, 'tensor', axis=1, tiled=True)  84.8 us
    dot_general x1, matrix products, per_device(): jnp.dot(up_grad, proj_upgrad.astype(jnp.bfloat16), preferred_element_type...  28.8 us
    another operation x1, other arithmetic  12.2 us
    dot_general x1, matrix products, per_device(): lax.dot_general(rows_all, queries, (((1,), (1,)), ((), ())), preferred_el...  9.49 us
    dot_general x1, matrix products, per_device(): jnp.dot(hidden, proj_hidden.astype(jnp.bfloat16), preferred_element_type=...  5.54 us
  transfers between devices with their start and end apart: 2, of which 2 were waited for; matrix products, arithmetic and copies ran while one was open for 3% of the time, Pallas kernels for 0%

commit v1 on v0

v1 whole, which is shorter than its diff:
```python
import functools

import jax
import jax.numpy as jnp
from jax import lax
from jax.experimental import pallas as pl
from jax.experimental.pallas import tpu as pltpu
from jax.sharding import PartitionSpec as P

EXAMPLES = 128
MESH = pl.DeviceIdType.MESH
PIECES = 3


def factors_kernel(
    n, chunks, scales,
    og_hbm, li_ref, gate_hbm, up_hbm, w_hbm, pin_ref, pout_ref, phid_ref, pupg_ref,
    out_ref,
    og, gate, up, w, phid, pupg, hid, upg, part, gathered, fact,
    local_sem, send_sem, recv_sem, sum_send, sum_recv, fact_send, fact_recv,
):
    depth = og_hbm.shape[0]
    rows = og.shape[1]
    ff = w.shape[0]
    rank = pin_ref.shape[0]
    lines = n // 4
    width = rows // chunks
    groups = n // 16
    share = width // groups
    me = lax.axis_index("tensor")
    z, y, c = me // 4, (me // 2) % 2, me % 2
    f32 = jnp.float32

    def block(zz, yy, cc):
        return (zz * 2 + yy) * 2 + cc

    loads = [
        pltpu.make_async_copy(og_hbm, og.at[pl.ds(pl.multiple_of(me * depth, 16), depth), :], local_sem.at[0]),
        pltpu.make_async_copy(gate_hbm, gate, local_sem.at[1]),
        pltpu.make_async_copy(up_hbm, up, local_sem.at[2]),
        pltpu.make_async_copy(w_hbm, w, local_sem.at[3]),
    ]
    for load in loads:
        load.start()

    barrier = pltpu.get_barrier_semaphore()

    @pl.loop(1, n)
    def _(step):
        pl.semaphore_signal(barrier, inc=1, device_id={"tensor": lax.rem(me + step, n)}, device_id_type=MESH)

    pl.semaphore_wait(barrier, n - 1)

    def lanes(k):
        return pl.ds(pl.multiple_of(k * width, 128), width)

    def copy(blk, k, slot, target):
        where = og.at[pl.ds(pl.multiple_of(blk * depth, 16), depth), lanes(k)]
        return pltpu.make_async_remote_copy(
            src_ref=where, dst_ref=where, send_sem=send_sem.at[slot, k], recv_sem=recv_sem.at[blk, k],
            device_id={"tensor": target}, device_id_type=MESH,
        )

    def to_core(blk, k):
        return copy(blk, k, blk // 2, block(z, y, 1 - c))

    def to_side(blk, k):
        return copy(blk, k, n // 2 + blk // 4, block(z, 1 - y, c))

    def to_next(blk, k):
        return copy(blk, k, n // 2 + lines + blk // 4, block(jnp.minimum(z + 1, lines - 1), y, c))

    def to_last(blk, k):
        return copy(blk, k, n // 2 + 2 * lines + blk // 4, block(jnp.maximum(z - 1, 0), y, c))

    def arrived(blk, k):
        to_core(blk, k).wait_recv()

    loads[0].wait()

    @pl.loop(0, chunks)
    def _(k):
        @pl.when(z < lines - 1)
        def _():
            to_next(me, k).start()

        @pl.when(z > 0)
        def _():
            to_last(me, k).start()

        to_side(me, k).start()
        to_core(me, k).start()

    def from_side(zz, k):
        blk = block(zz, 1 - y, c)
        arrived(blk, k)
        to_core(blk, k).start()

    def stage(d, k):
        if d < lines:
            @pl.when(z >= d)
            def _():
                blk = block(z - d, y, c)
                arrived(blk, k)

                @pl.when(z < lines - 1)
                def _():
                    to_next(blk, k).start()

                to_side(blk, k).start()
                to_core(blk, k).start()

            @pl.when(z + d < lines)
            def _():
                blk = block(z + d, y, c)
                arrived(blk, k)

                @pl.when(z > 0)
                def _():
                    to_last(blk, k).start()

                to_side(blk, k).start()
                to_core(blk, k).start()

        e = d - 1

        @pl.when(z >= e)
        def _():
            from_side(z - e, k)

        if e > 0:
            @pl.when(z + e < lines)
            def _():
                from_side(z + e, k)

    phid[...] = phid_ref[...].astype(f32).astype(jnp.bfloat16)
    pupg[...] = pupg_ref[...].astype(f32).astype(jnp.bfloat16)
    part[pl.ds(0, rank), :] = jnp.dot(
        pin_ref[...].astype(f32).astype(jnp.bfloat16), li_ref[...], preferred_element_type=f32
    ).astype(jnp.bfloat16)
    mine = og[pl.ds(pl.multiple_of(me * depth, 16), depth), :]
    part[pl.ds(3 * rank, rank), :] = jnp.dot(
        pout_ref[...].astype(f32).astype(jnp.bfloat16), mine, preferred_element_type=f32
    ).astype(jnp.bfloat16)
    for load in loads[1:]:
        load.wait()

    tile = ff // PIECES

    def multiply(t, k):
        at = pl.ds(t * tile, tile)
        grad = jnp.dot(w[at, :], og[:, lanes(k)], preferred_element_type=f32)
        pre = gate[at, lanes(k)].astype(f32)
        act = pre / (1.0 + jnp.exp(-pre))
        hid[at, :] = (act * up[at, lanes(k)].astype(f32)).astype(jnp.bfloat16)
        upg[at, :] = (grad * act).astype(jnp.bfloat16)

    def spot(owner, k):
        return (
            pl.ds(pl.multiple_of((owner // groups) * 16, 16), 16),
            pl.ds(pl.multiple_of(k * width + (owner % groups) * share, 128), share),
        )

    def held(k):
        return pl.ds(pl.multiple_of(k * share, 128), share)

    def sum_copy(other, source, k):
        return pltpu.make_async_remote_copy(
            src_ref=part.at[spot(other, k)], dst_ref=gathered.at[source, :, held(k)],
            send_sem=sum_send.at[other, k], recv_sem=sum_recv.at[source, k],
            device_id={"tensor": other}, device_id_type=MESH,
        )

    def fact_copy(other, owner, k):
        return pltpu.make_async_remote_copy(
            src_ref=fact.at[spot(owner, k)], dst_ref=fact.at[spot(owner, k)],
            send_sem=fact_send.at[other, k], recv_sem=fact_recv.at[owner, k],
            device_id={"tensor": other}, device_id_type=MESH,
        )

    def project(k):
        part[pl.ds(rank, rank), lanes(k)] = jnp.dot(
            phid[...], hid[...], preferred_element_type=f32
        ).astype(jnp.bfloat16)
        part[pl.ds(2 * rank, rank), lanes(k)] = jnp.dot(
            pupg[...], upg[...], preferred_element_type=f32
        ).astype(jnp.bfloat16)

        @pl.loop(1, n)
        def _(step):
            sum_copy(lax.rem(me + step, n), me, k).start()

    def add_up(k):
        gathered[pl.ds(me, 1), :, held(k)] = part[spot(me, k)][None]

        @pl.loop(1, n)
        def _(step):
            other = lax.rem(me + step, n)
            sum_copy(other, other, k).wait_recv()

        total = jnp.zeros((16, share), f32)
        for i in range(n):
            total = total + gathered[i, :, held(k)].astype(f32)
        which = (me // groups) * 16 // rank
        scale = jnp.where((which == 0) | (which == 3), scales[0], scales[1]).astype(f32)
        fact[spot(me, k)] = (total * scale).astype(jnp.bfloat16)

        @pl.loop(1, n)
        def _(step):
            fact_copy(lax.rem(me + step, n), me, k).start()

    @pl.loop(0, chunks + 2)
    def _(k):
        computing = (k > 0) & (k <= chunks)
        for d in range(1, lines + 1):
            @pl.when(k < chunks)
            def _(d=d):
                stage(d, k)

            if d <= PIECES:
                @pl.when(computing)
                def _(d=d):
                    multiply(d - 1, k - 1)

            if d == PIECES:
                @pl.when(computing)
                def _():
                    project(k - 1)

        @pl.when(k > 1)
        def _():
            add_up(k - 2)

        @pl.when(k < chunks)
        def _():
            @pl.loop(0, n // 2)
            def _(chip):
                arrived(chip * 2 + 1 - c, k)

    @pl.loop(0, chunks)
    def _(k):
        @pl.loop(1, n)
        def _(step):
            other = lax.rem(me + step, n)
            fact_copy(other, other, k).wait_recv()
            fact_copy(other, me, k).wait_send()
            sum_copy(other, me, k).wait_send()

        @pl.loop(0, n // 2)
        def _(chip):
            to_core(chip * 2 + c, k).wait_send()

        @pl.loop(0, lines)
        def _(zz):
            blk = block(zz, y, c)
            to_side(blk, k).wait_send()

            @pl.when((zz <= z) & (z < lines - 1))
            def _():
                to_next(blk, k).wait_send()

            @pl.when((zz >= z) & (z > 0))
            def _():
                to_last(blk, k).wait_send()

    out_ref[...] = fact[...]


def scores_kernel(fact_ref, queries_ref, ids_ref, out_ref, kron, wide):
    rank = fact_ref.shape[0] // 4
    width = fact_ref.shape[1]
    f32 = jnp.float32
    wide[...] = fact_ref[...].astype(f32)
    for half, (a, b) in enumerate(((0, 2), (1, 3))):
        right = wide[pl.ds(b * rank, rank), :]
        for i in range(rank):
            left = wide[pl.ds(a * rank + i, 1), :]
            kron[pl.ds((half * rank + i) * rank, rank), :] = (left * right).astype(jnp.bfloat16)
    rows = jnp.dot(queries_ref[...], kron[...], preferred_element_type=f32)
    onehot = (
        lax.broadcasted_iota(jnp.int32, (EXAMPLES, width), 0) == ids_ref[...]
    ).astype(f32).astype(jnp.bfloat16)
    total = jnp.zeros(out_ref.shape, f32)
    rest = rows
    for _ in range(3):
        top = rest.astype(jnp.bfloat16)
        total = total + lax.dot_general(onehot, top, (((1,), (1,)), ((), ())), preferred_element_type=f32)
        rest = rest - top.astype(f32)

    @pl.when(pl.program_id(0) == 0)
    def _():
        out_ref[...] = total

    @pl.when(pl.program_id(0) > 0)
    def _():
        out_ref[...] += total


def per_device(
    n, layer_input, out_grad, gate_pre, up_pre, down_weight,
    proj_input, proj_output, proj_hidden, proj_upgrad, queries, example_ids,
):
    rows, depth = out_grad.shape
    ff, d = down_weight.shape
    rank = proj_input.shape[1]
    chunks = 4 if n <= 16 else 2
    width = rows // chunks
    groups = n // 16
    scales = ((1.5 / d) ** 0.5, (1.5 / (ff * n)) ** 0.5)
    bf16 = jnp.bfloat16
    vmem = pl.BlockSpec(memory_space=pltpu.VMEM)
    hbm = pl.BlockSpec(memory_space=pl.ANY)
    sems = pltpu.SemaphoreType.DMA
    fact = pl.pallas_call(
        functools.partial(factors_kernel, n, chunks, scales),
        out_shape=jax.ShapeDtypeStruct((4 * rank, rows), bf16),
        in_specs=[hbm, vmem, hbm, hbm, hbm, vmem, vmem, vmem, vmem],
        out_specs=vmem,
        scratch_shapes=[
            pltpu.VMEM((d, rows), bf16),
            pltpu.VMEM((ff, rows), bf16),
            pltpu.VMEM((ff, rows), bf16),
            pltpu.VMEM((ff, d), bf16),
            pltpu.VMEM((rank, ff), bf16),
            pltpu.VMEM((rank, ff), bf16),
            pltpu.VMEM((ff, width), bf16),
            pltpu.VMEM((ff, width), bf16),
            pltpu.VMEM((4 * rank, rows), bf16),
            pltpu.VMEM((n, 16, rows // groups), bf16),
            pltpu.VMEM((4 * rank, rows), bf16),
            sems((4,)),
            sems((n // 2 + 3 * (n // 4), chunks)),
            sems((n, chunks)),
            sems((n, chunks)),
            sems((n, chunks)),
            sems((n, chunks)),
            sems((n, chunks)),
        ],
        compiler_params=pltpu.CompilerParams(
            collective_id=0, has_side_effects=True, vmem_limit_bytes=56 * 2**20
        ),
        cost_estimate=pl.CostEstimate(
            flops=2 * rows * ff * d, bytes_accessed=2 * ff * d, transcendentals=rows * ff
        ),
    )(
        out_grad.T, layer_input.T, gate_pre.T, up_pre.T, down_weight,
        proj_input.T, proj_output.T, proj_hidden.T, proj_upgrad.T,
    )
    count = queries.shape[0]
    step = rows // 4
    return pl.pallas_call(
        scores_kernel,
        grid=(4,),
        out_shape=jax.ShapeDtypeStruct((EXAMPLES, count), jnp.float32),
        in_specs=[
            pl.BlockSpec((4 * rank, step), lambda i: (0, i)),
            pl.BlockSpec(queries.shape, lambda i: (0, 0)),
            pl.BlockSpec((1, step), lambda i: (0, i)),
        ],
        out_specs=pl.BlockSpec((EXAMPLES, count), lambda i: (0, 0)),
        scratch_shapes=[
            pltpu.VMEM((2 * rank * rank, step), bf16),
            pltpu.VMEM((4 * rank, step), jnp.float32),
        ],
        compiler_params=pltpu.CompilerParams(vmem_limit_bytes=32 * 2**20),
    )(fact, queries, example_ids[None, :])


def solution(mesh):
    split = P("parts", "tensor")
    rows = P("tensor", None)
    placed = (split,) * 4 + (rows,) * 6 + (P("parts"),)
    return jax.shard_map(
        functools.partial(per_device, mesh.shape["tensor"]),
        mesh=mesh, in_specs=placed, out_specs=split, check_vma=False,
    )
```

time: 253 us -> 117 us (0.46)
  waiting for transfers between devices: 177 us -> 0 us
  Pallas kernels: 0 us -> 115 us
  matrix products: 47.6 us -> 0 us
  other arithmetic: 14.7 us -> 0 us
  between operations: 13.5 us -> 0.03 us
    pallas_call x0 -> x2, Pallas kernels: none -> 115 us  [the longest x1 108 us: per_device(): pl.pallas_call(functools.partial(factors_kernel, n, chunks, scales), out_...]
    psum x1 -> x0, waiting for transfers between devices: 91.7 us -> none  [per_device(): summed = lax.psum(partial_value, 'tensor')]
    all_gather x1 -> x0, waiting for transfers between devices: 84.8 us -> none  [per_device(): lax.all_gather(out_grad, 'tensor', axis=1, tiled=True)]
    dot_general x6 -> x0, matrix products: 47.6 us -> none  [the longest x1 28.8 us: per_device(): jnp.dot(up_grad, proj_upgrad.astype(jnp.bfloat16), preferred_element_type...]
    another operation x1 -> x0, other arithmetic: 12.2 us -> none
  transfers between devices with their start and end apart: 2 -> 0, of which waited for: 2 -> 0; matrix products, arithmetic and copies ran while one was open for 3% -> 0% of each run, Pallas kernels for 0% -> 0%
where the time goes in v1:
time: 117 us; the launch traced here: 116 us
  Pallas kernels  115 us (98%)
    pallas_call x1, Pallas kernels, per_device(): pl.pallas_call(functools.partial(factors_kernel, n, chunks, scales), out_...  108 us
    pallas_call x1, Pallas kernels, per_device(): pl.pallas_call(scores_kernel, grid=(4,), out_shape=jax.ShapeDtypeStruct((...  7.33 us

profile of v1, /device:TPU:0, one launch (start us, length us, event | category | flops | bytes accessed | tf_op | source)
XLA Modules:
  0.0 116.5 jit_solution(15044863493130631742)
XLA Ops:
  0.0 0.0 copy-start
  0.0 0.0 copy-start.2
  0.0 108.1 %shard_map.109.fact_ref = bf16[256,1024]{1,0:T(8,128)(2,1)} custom-call(bf16[320,1024]{1,0:T(8,128)(2,1)} %bitcast.12, bf16[320,1024]{1,0:T(8,128)(2,1)} %bitcast.13, bf16[1728,1024]{1,0:T(8,128)(2,1)} %bitcast.10, bf16[1728,1024]{1,0:T(8,128)(2,1)} %bitcast.11, bf16[1728,5120]{1,0:T(8,128)(2,1)} %w_hbm.1, s32[64,320]{1,0:T(8,128)} %bitcast.16, ...), custom_call_target="tpu_custom_call" | custom-call | flops 18119393280 | bytes 17694720 | tf_op jit(solution)/shard_map/pallas_call | solution.py:314
  108.1 0.0 copy-done
  108.1 0.0 copy-done.2
  108.1 0.0 copy-start.1
  108.1 1.0 copy-done.1
  109.1 7.3 %shard_map.110 = f32[128,256]{1,0:T(8,128)} custom-call(bf16[256,1024]{1,0:T(8,128)(2,1)S(1)} %copy-done.1, bf16[256,8192]{1,0:T(8,128)(2,1)S(1)} %copy-done, s32[1,1024]{1,0:T(1,128)S(1)} %bitcast.9), custom_call_target="tpu_custom_call" | custom-call | tf_op jit(solution)/shard_map/pallas_call | solution.py:351
Async XLA Ops:
  0.0 108.1 %copy-start = (bf16[256,8192]{1,0:T(8,128)(2,1)S(1)}, bf16[256,8192]{1,0:T(8,128)(2,1)}, u32[]{:S(2)}) copy-start(bf16[256,8192]{1,0:T(8,128)(2,1)} %queries_ref.1) | copy-start | bytes 12582916
  0.0 108.1 %copy-start.2 = (s32[1024]{0:T(1024)S(1)}, s32[1024]{0:T(1024)}, u32[]{:S(2)}) copy-start(s32[1024]{0:T(1024)} %param.21) | copy-start | bytes 12292
  108.1 1.0 copy-start.1

commit v2 on v1

--- a/solution.py
+++ b/solution.py
@@ -142,8 +142,6 @@
     part[pl.ds(3 * rank, rank), :] = jnp.dot(
         pout_ref[...].astype(f32).astype(jnp.bfloat16), mine, preferred_element_type=f32
     ).astype(jnp.bfloat16)
-    for load in loads[1:]:
-        load.wait()
 
     tile = ff // PIECES
 
@@ -217,6 +215,18 @@
             def _(d=d):
                 stage(d, k)
 
+            if d == 1:
+                @pl.when(k == 1)
+                def _():
+                    for load in loads[1:]:
+                        load.wait()
+
+                @pl.when(computing)
+                def _():
+                    @pl.loop(0, n // 2)
+                    def _(chip):
+                        arrived(chip * 2 + 1 - c, k - 1)
+
             if d <= PIECES:
                 @pl.when(computing)
                 def _(d=d):
@@ -230,12 +240,6 @@
         @pl.when(k > 1)
         def _():
             add_up(k - 2)
-
-        @pl.when(k < chunks)
-        def _():
-            @pl.loop(0, n // 2)
-            def _(chip):
-                arrived(chip * 2 + 1 - c, k)
 
     @pl.loop(0, chunks)
     def _(k):

time: 117 us -> 114 us (0.974)
  Pallas kernels: 115 us -> 112 us
    pallas_call x1, Pallas kernels: 108 us -> 105 us  [per_device(): pl.pallas_call(functools.partial(factors_kernel, n, chunks, scales), out_...]
where the time goes in v2:
time: 114 us; the launch traced here: 113 us
  Pallas kernels  112 us (98%)
    pallas_call x1, Pallas kernels, per_device(): pl.pallas_call(functools.partial(factors_kernel, n, chunks, scales), out_...  105 us
    pallas_call x1, Pallas kernels, per_device(): pl.pallas_call(scores_kernel, grid=(4,), out_shape=jax.ShapeDtypeStruct((...  7.35 us

profile of v2, /device:TPU:0, one launch (start us, length us, event | category | flops | bytes accessed | tf_op | source)
XLA Modules:
  0.0 113.4 jit_solution(6173002985753621546)
XLA Ops:
  0.0 0.0 copy-start
  0.0 0.0 copy-start.2
  0.0 105.0 %shard_map.109.fact_ref = bf16[256,1024]{1,0:T(8,128)(2,1)} custom-call(bf16[320,1024]{1,0:T(8,128)(2,1)} %bitcast.12, bf16[320,1024]{1,0:T(8,128)(2,1)} %bitcast.13, bf16[1728,1024]{1,0:T(8,128)(2,1)} %bitcast.10, bf16[1728,1024]{1,0:T(8,128)(2,1)} %bitcast.11, bf16[1728,5120]{1,0:T(8,128)(2,1)} %w_hbm.1, s32[64,320]{1,0:T(8,128)} %bitcast.16, ...), custom_call_target="tpu_custom_call" | custom-call | flops 18119393280 | bytes 17694720 | tf_op jit(solution)/shard_map/pallas_call | solution.py:318
  105.0 0.0 copy-done
  105.0 0.0 copy-done.2
  105.0 0.0 copy-start.1
  105.1 1.0 copy-done.1
  106.1 7.4 %shard_map.110 = f32[128,256]{1,0:T(8,128)} custom-call(bf16[256,1024]{1,0:T(8,128)(2,1)S(1)} %copy-done.1, bf16[256,8192]{1,0:T(8,128)(2,1)S(1)} %copy-done, s32[1,1024]{1,0:T(1,128)S(1)} %bitcast.9), custom_call_target="tpu_custom_call" | custom-call | tf_op jit(solution)/shard_map/pallas_call | solution.py:355
Async XLA Ops:
  0.0 105.0 %copy-start = (bf16[256,8192]{1,0:T(8,128)(2,1)S(1)}, bf16[256,8192]{1,0:T(8,128)(2,1)}, u32[]{:S(2)}) copy-start(bf16[256,8192]{1,0:T(8,128)(2,1)} %queries_ref.1) | copy-start | bytes 12582916
  0.0 105.0 %copy-start.2 = (s32[1024]{0:T(1024)S(1)}, s32[1024]{0:T(1024)}, u32[]{:S(2)}) copy-start(s32[1024]{0:T(1024)} %param.21) | copy-start | bytes 12292
  105.0 1.0 copy-start.1

commit v3 on v2

--- a/solution.py
+++ b/solution.py
@@ -78,8 +78,7 @@
 
     loads[0].wait()
 
-    @pl.loop(0, chunks)
-    def _(k):
+    def send_own(k):
         @pl.when(z < lines - 1)
         def _():
             to_next(me, k).start()
@@ -90,6 +89,8 @@
 
         to_side(me, k).start()
         to_core(me, k).start()
+
+    send_own(0)
 
     def from_side(zz, k):
         blk = block(zz, 1 - y, c)
@@ -214,6 +215,11 @@
             @pl.when(k < chunks)
             def _(d=d):
                 stage(d, k)
+
+            if d == 2:
+                @pl.when(k + 1 < chunks)
+                def _():
+                    send_own(k + 1)
 
             if d == 1:
                 @pl.when(k == 1)

time: 114 us -> 107 us (0.939)
  Pallas kernels: 112 us -> 106 us
    pallas_call x1, Pallas kernels: 105 us -> 98.7 us  [per_device(): pl.pallas_call(functools.partial(factors_kernel, n, chunks, scales), out_...]
where the time goes in v3:
time: 107 us
  Pallas kernels  106 us (99%)
    pallas_call x1, Pallas kernels, per_device(): pl.pallas_call(functools.partial(factors_kernel, n, chunks, scales), out_...  98.7 us
    pallas_call x1, Pallas kernels, per_device(): pl.pallas_call(scores_kernel, grid=(4,), out_shape=jax.ShapeDtypeStruct((...  7.33 us

profile of v3, /device:TPU:0, one launch (start us, length us, event | category | flops | bytes accessed | tf_op | source)
XLA Modules:
  0.0 107.1 jit_solution(12782025136831880946)
XLA Ops:
  0.0 0.0 copy-start
  0.0 0.0 copy-start.2
  0.0 98.7 %shard_map.109.fact_ref = bf16[256,1024]{1,0:T(8,128)(2,1)} custom-call(bf16[320,1024]{1,0:T(8,128)(2,1)} %bitcast.12, bf16[320,1024]{1,0:T(8,128)(2,1)} %bitcast.13, bf16[1728,1024]{1,0:T(8,128)(2,1)} %bitcast.10, bf16[1728,1024]{1,0:T(8,128)(2,1)} %bitcast.11, bf16[1728,5120]{1,0:T(8,128)(2,1)} %w_hbm.1, s32[64,320]{1,0:T(8,128)} %bitcast.16, ...), custom_call_target="tpu_custom_call" | custom-call | flops 18119393280 | bytes 17694720 | tf_op jit(solution)/shard_map/pallas_call | solution.py:324
  98.7 0.0 copy-done
  98.8 0.0 copy-done.2
  98.8 0.0 copy-start.1
  98.8 1.0 copy-done.1
  99.8 7.3 %shard_map.110 = f32[128,256]{1,0:T(8,128)} custom-call(bf16[256,1024]{1,0:T(8,128)(2,1)S(1)} %copy-done.1, bf16[256,8192]{1,0:T(8,128)(2,1)S(1)} %copy-done, s32[1,1024]{1,0:T(1,128)S(1)} %bitcast.9), custom_call_target="tpu_custom_call" | custom-call | tf_op jit(solution)/shard_map/pallas_call | solution.py:361
Async XLA Ops:
  0.0 98.7 %copy-start = (bf16[256,8192]{1,0:T(8,128)(2,1)S(1)}, bf16[256,8192]{1,0:T(8,128)(2,1)}, u32[]{:S(2)}) copy-start(bf16[256,8192]{1,0:T(8,128)(2,1)} %queries_ref.1) | copy-start | bytes 12582916
  0.0 98.8 %copy-start.2 = (s32[1024]{0:T(1024)S(1)}, s32[1024]{0:T(1024)}, u32[]{:S(2)}) copy-start(s32[1024]{0:T(1024)} %param.21) | copy-start | bytes 12292
  98.8 1.0 copy-start.1

commit v4 on v3

--- a/solution.py
+++ b/solution.py
@@ -15,8 +15,8 @@
 def factors_kernel(
     n, chunks, scales,
     og_hbm, li_ref, gate_hbm, up_hbm, w_hbm, pin_ref, pout_ref, phid_ref, pupg_ref,
-    out_ref,
-    og, gate, up, w, phid, pupg, hid, upg, part, gathered, fact,
+    queries_hbm, ids_ref, out_ref,
+    og, gate, up, w, phid, pupg, hid, upg, part, gathered, fact, queries, kron, wide,
     local_sem, send_sem, recv_sem, sum_send, sum_recv, fact_send, fact_recv,
 ):
     depth = og_hbm.shape[0]
@@ -39,6 +39,7 @@
         pltpu.make_async_copy(gate_hbm, gate, local_sem.at[1]),
         pltpu.make_async_copy(up_hbm, up, local_sem.at[2]),
         pltpu.make_async_copy(w_hbm, w, local_sem.at[3]),
+        pltpu.make_async_copy(queries_hbm, queries, local_sem.at[4]),
     ]
     for load in loads:
         load.start()
@@ -208,7 +209,34 @@
         def _(step):
             fact_copy(lax.rem(me + step, n), me, k).start()
 
-    @pl.loop(0, chunks + 2)
+    out_ref[...] = jnp.zeros(out_ref.shape, f32)
+
+    def score(k):
+        @pl.loop(1, n)
+        def _(step):
+            other = lax.rem(me + step, n)
+            fact_copy(other, other, k).wait_recv()
+
+        wide[...] = fact[:, lanes(k)].astype(f32)
+        for half, (a, b) in enumerate(((0, 2), (1, 3))):
+            right = wide[pl.ds(b * rank, rank), :]
+            for i in range(rank):
+                left = wide[pl.ds(a * rank + i, 1), :]
+                kron[pl.ds((half * rank + i) * rank, rank), :] = (left * right).astype(jnp.bfloat16)
+        rest = jnp.dot(queries[...], kron[...], preferred_element_type=f32)
+        onehot = (
+            lax.broadcasted_iota(jnp.int32, (EXAMPLES, width), 0) == ids_ref[:, lanes(k)]
+        ).astype(f32).astype(jnp.bfloat16)
+        total = jnp.zeros(out_ref.shape, f32)
+        for _ in range(3):
+            top = rest.astype(jnp.bfloat16)
+            total = total + lax.dot_general(
+                onehot, top, (((1,), (1,)), ((), ())), preferred_element_type=f32
+            )
+            rest = rest - top.astype(f32)
+        out_ref[...] += total
+
+    @pl.loop(0, chunks + 3)
     def _(k):
         computing = (k > 0) & (k <= chunks)
         for d in range(1, lines + 1):
@@ -243,16 +271,19 @@
                 def _():
                     project(k - 1)
 
-        @pl.when(k > 1)
+        @pl.when((k > 1) & (k < chunks + 2))
         def _():
             add_up(k - 2)
+
+        @pl.when(k > 2)
+        def _():
+            score(k - 3)
 
     @pl.loop(0, chunks)
     def _(k):
         @pl.loop(1, n)
         def _(step):
             other = lax.rem(me + step, n)
-            fact_copy(other, other, k).wait_recv()
             fact_copy(other, me, k).wait_send()
             sum_copy(other, me, k).wait_send()
 
@@ -272,38 +303,6 @@
             @pl.when((zz >= z) & (z > 0))
             def _():
                 to_last(blk, k).wait_send()
-
-    out_ref[...] = fact[...]
-
-
-def scores_kernel(fact_ref, queries_ref, ids_ref, out_ref, kron, wide):
-    rank = fact_ref.shape[0] // 4
-    width = fact_ref.shape[1]
-    f32 = jnp.float32
-    wide[...] = fact_ref[...].astype(f32)
-    for half, (a, b) in enumerate(((0, 2), (1, 3))):
-        right = wide[pl.ds(b * rank, rank), :]
-        for i in range(rank):
-            left = wide[pl.ds(a * rank + i, 1), :]
-            kron[pl.ds((half * rank + i) * rank, rank), :] = (left * right).astype(jnp.bfloat16)
-    rows = jnp.dot(queries_ref[...], kron[...], preferred_element_type=f32)
-    onehot = (
-        lax.broadcasted_iota(jnp.int32, (EXAMPLES, width), 0) == ids_ref[...]
-    ).astype(f32).astype(jnp.bfloat16)
-    total = jnp.zeros(out_ref.shape, f32)
-    rest = rows
-    for _ in range(3):
-        top = rest.astype(jnp.bfloat16)
-        total = total + lax.dot_general(onehot, top, (((1,), (1,)), ((), ())), preferred_element_type=f32)
-        rest = rest - top.astype(f32)
-
-    @pl.when(pl.program_id(0) == 0)
-    def _():
-        out_ref[...] = total
-
-    @pl.when(pl.program_id(0) > 0)
-    def _():
-        out_ref[...] += total
 
 
 def per_device(
@@ -321,10 +320,11 @@
     vmem = pl.BlockSpec(memory_space=pltpu.VMEM)
     hbm = pl.BlockSpec(memory_space=pl.ANY)
     sems = pltpu.SemaphoreType.DMA
-    fact = pl.pallas_call(
+    count = queries.shape[0]
+    return pl.pallas_call(
         functools.partial(factors_kernel, n, chunks, scales),
-        out_shape=jax.ShapeDtypeStruct((4 * rank, rows), bf16),
-        in_specs=[hbm, vmem, hbm, hbm, hbm, vmem, vmem, vmem, vmem],
+        out_shape=jax.ShapeDtypeStruct((EXAMPLES, count), jnp.float32),
+        in_specs=[hbm, vmem, hbm, hbm, hbm, vmem, vmem, vmem, vmem, hbm, vmem],
         out_specs=vmem,
         scratch_shapes=[
             pltpu.VMEM((d, rows), bf16),
@@ -338,7 +338,10 @@
             pltpu.VMEM((4 * rank, rows), bf16),
             pltpu.VMEM((n, 16, rows // groups), bf16),
             pltpu.VMEM((4 * rank, rows), bf16),
-            sems((4,)),
+            pltpu.VMEM(queries.shape, bf16),
+            pltpu.VMEM((queries.shape[1], width), bf16),
+            pltpu.VMEM((4 * rank, width), jnp.float32),
+            sems((5,)),
             sems((n // 2 + 3 * (n // 4), chunks)),
             sems((n, chunks)),
             sems((n, chunks)),
@@ -355,25 +358,8 @@
     )(
         out_grad.T, layer_input.T, gate_pre.T, up_pre.T, down_weight,
         proj_input.T, proj_output.T, proj_hidden.T, proj_upgrad.T,
+        queries, example_ids[None, :],
     )
-    count = queries.shape[0]
-    step = rows // 4
-    return pl.pallas_call(
-        scores_kernel,
-        grid=(4,),
-        out_shape=jax.ShapeDtypeStruct((EXAMPLES, count), jnp.float32),
-        in_specs=[
-            pl.BlockSpec((4 * rank, step), lambda i: (0, i)),
-            pl.BlockSpec(queries.shape, lambda i: (0, 0)),
-            pl.BlockSpec((1, step), lambda i: (0, i)),
-        ],
-        out_specs=pl.BlockSpec((EXAMPLES, count), lambda i: (0, 0)),
-        scratch_shapes=[
-            pltpu.VMEM((2 * rank * rank, step), bf16),
-            pltpu.VMEM((4 * rank, step), jnp.float32),
-        ],
-        compiler_params=pltpu.CompilerParams(vmem_limit_bytes=32 * 2**20),
-    )(fact, queries, example_ids[None, :])
 
 
 def solution(mesh):

time: 107 us -> 104 us (0.972)
  Pallas kernels: 106 us -> 102 us
    pallas_call x1 -> x0, Pallas kernels: 7.33 us -> none  [per_device(): pl.pallas_call(scores_kernel, grid=(4,), out_shape=jax.ShapeDtypeStruct((...]
    pallas_call x1, Pallas kernels: 98.7 us -> 102 us  [per_device(): pl.pallas_call(functools.partial(factors_kernel, n, chunks, scales), out_...]
where the time goes in v4:
time: 104 us
  Pallas kernels  102 us (98%)
  local copies, waits for them, and re-layouts  1.57 us (2%)
    pallas_call x1, Pallas kernels, per_device(): pl.pallas_call(functools.partial(factors_kernel, n, chunks, scales), out_...  102 us

profile of v4, /device:TPU:0, one launch (start us, length us, event | category | flops | bytes accessed | tf_op | source)
XLA Modules:
  0.0 103.9 jit_solution(1384613433494821702)
XLA Ops:
  0.0 102.3 %shard_map.109 = f32[128,256]{1,0:T(8,128)} custom-call(bf16[320,1024]{1,0:T(8,128)(2,1)} %bitcast.11, bf16[320,1024]{1,0:T(8,128)(2,1)} %bitcast.12, bf16[1728,1024]{1,0:T(8,128)(2,1)} %bitcast.9, bf16[1728,1024]{1,0:T(8,128)(2,1)} %bitcast.10, bf16[1728,5120]{1,0:T(8,128)(2,1)} %w_hbm.1, s32[64,320]{1,0:T(8,128)} %bitcast.15, s32[64,320]{1,0:T(8,128)} %bitcast.16, ...), custom_call_target="tpu_custom_call" | custom-call | flops 18119393280 | bytes 17694720 | tf_op jit(solution)/shard_map/pallas_call | solution.py:324
  102.3 1.6 %copy.13 = f32[128,256]{1,0:T(8,128)} copy(f32[128,256]{1,0:T(8,128)} %shard_map.109) | data formatting | bytes 262144

commit v5 on v4

--- a/solution.py
+++ b/solution.py
@@ -69,10 +69,10 @@
         return copy(blk, k, n // 2 + blk // 4, block(z, 1 - y, c))
 
     def to_next(blk, k):
-        return copy(blk, k, n // 2 + lines + blk // 4, block(jnp.minimum(z + 1, lines - 1), y, c))
+        return copy(blk, k, n // 2 + lines + blk // 2, block(jnp.minimum(z + 1, lines - 1), y, c))
 
     def to_last(blk, k):
-        return copy(blk, k, n // 2 + 2 * lines + blk // 4, block(jnp.maximum(z - 1, 0), y, c))
+        return copy(blk, k, n + lines + blk // 2, block(jnp.maximum(z - 1, 0), y, c))
 
     def arrived(blk, k):
         to_core(blk, k).wait_recv()
@@ -134,6 +134,31 @@
             @pl.when(z + e < lines)
             def _():
                 from_side(z + e, k)
+
+    def side_first(d, k):
+        def on(blk, up, down):
+            arrived(blk, k)
+            if up:
+                @pl.when(z < lines - 1)
+                def _():
+                    to_next(blk, k).start()
+            if down:
+                @pl.when(z > 0)
+                def _():
+                    to_last(blk, k).start()
+            to_core(blk, k).start()
+
+        if d == 1:
+            on(block(z, 1 - y, c), True, True)
+        if d < lines:
+            for yy in (y, 1 - y):
+                @pl.when(z >= d)
+                def _(yy=yy):
+                    on(block(z - d, yy, c), True, False)
+
+                @pl.when(z + d < lines)
+                def _(yy=yy):
+                    on(block(z + d, yy, c), False, True)
 
     phid[...] = phid_ref[...].astype(f32).astype(jnp.bfloat16)
     pupg[...] = pupg_ref[...].astype(f32).astype(jnp.bfloat16)
@@ -240,7 +265,11 @@
     def _(k):
         computing = (k > 0) & (k <= chunks)
         for d in range(1, lines + 1):
-            @pl.when(k < chunks)
+            @pl.when(k == 0)
+            def _(d=d):
+                side_first(d, k)
+
+            @pl.when((k > 0) & (k < chunks))
             def _(d=d):
                 stage(d, k)
 
@@ -294,15 +323,27 @@
         @pl.loop(0, lines)
         def _(zz):
             blk = block(zz, y, c)
-            to_side(blk, k).wait_send()
+            across = block(zz, 1 - y, c)
+
+            @pl.when((k > 0) | (zz == z))
+            def _():
+                to_side(blk, k).wait_send()
 
             @pl.when((zz <= z) & (z < lines - 1))
             def _():
                 to_next(blk, k).wait_send()
 
+                @pl.when(k == 0)
+                def _():
+                    to_next(across, k).wait_send()
+
             @pl.when((zz >= z) & (z > 0))
             def _():
                 to_last(blk, k).wait_send()
+
+                @pl.when(k == 0)
+                def _():
+                    to_last(across, k).wait_send()
 
 
 def per_device(
@@ -342,7 +383,7 @@
             pltpu.VMEM((queries.shape[1], width), bf16),
             pltpu.VMEM((4 * rank, width), jnp.float32),
             sems((5,)),
-            sems((n // 2 + 3 * (n // 4), chunks)),
+            sems((3 * (n // 2) + n // 4, chunks)),
             sems((n, chunks)),
             sems((n, chunks)),
             sems((n, chunks)),

time: 104 us -> 113 us (1.087)
  Pallas kernels: 102 us -> 111 us
    pallas_call x1, Pallas kernels: 102 us -> 111 us  [per_device(): pl.pallas_call(functools.partial(factors_kernel, n, chunks, scales), out_...]
where the time goes in v5:
time: 113 us; the launch traced here: 112 us
  Pallas kernels  111 us (98%)
  local copies, waits for them, and re-layouts  1.57 us (1%)
    pallas_call x1, Pallas kernels, per_device(): pl.pallas_call(functools.partial(factors_kernel, n, chunks, scales), out_...  111 us

profile of v5, /device:TPU:0, one launch (start us, length us, event | category | flops | bytes accessed | tf_op | source)
XLA Modules:
  0.0 112.5 jit_solution(9889178282412314459)
XLA Ops:
  0.0 110.9 %shard_map.109 = f32[128,256]{1,0:T(8,128)} custom-call(bf16[320,1024]{1,0:T(8,128)(2,1)} %bitcast.11, bf16[320,1024]{1,0:T(8,128)(2,1)} %bitcast.12, bf16[1728,1024]{1,0:T(8,128)(2,1)} %bitcast.9, bf16[1728,1024]{1,0:T(8,128)(2,1)} %bitcast.10, bf16[1728,5120]{1,0:T(8,128)(2,1)} %w_hbm.1, s32[64,320]{1,0:T(8,128)} %bitcast.15, s32[64,320]{1,0:T(8,128)} %bitcast.16, ...), custom_call_target="tpu_custom_call" | custom-call | flops 18119393280 | bytes 17694720 | tf_op jit(solution)/shard_map/pallas_call | solution.py:365
  110.9 1.6 %copy.13 = f32[128,256]{1,0:T(8,128)} copy(f32[128,256]{1,0:T(8,128)} %shard_map.109) | data formatting | bytes 262144
